TPU v7x, 32 devices: a whole 2x2x4 slice. The times are simulated.
32 devices in a mesh: dp: 8 (over z, y), tensor: 4 (over x, core).
Axes of the slice: x: 2, y: 2, z: 4, core: 2. Of those that a mesh axis runs over, the one named last changes fastest.
Arguments:
- output_gradient: bfloat16 [3072, 8192], P(('dp', 'tensor')), may hold values from -6 to 6
- attention_output: bfloat16 [3072, 8192], P('dp', 'tensor'), may hold values from -0.29882812 to 0.29882812
- frozen_projection: bfloat16 [8192, 8192], P('tensor', 'dp'), may hold values from -0.0625 to 0.0625
- domain_down_map: bfloat16 [4, 32, 8192], P(None, None, 'tensor'), may hold values from -0.29882812 to 0.29882812
- domain_up_map: bfloat16 [4, 32, 8192], P(None, None, 'tensor'), may hold values from -0.0625 to 0.0625
- common_down_map: bfloat16 [16, 8192], P(None, 'tensor'), may hold values from -0.29882812 to 0.29882812
- common_up_map: bfloat16 [16, 8192], P(None, 'tensor'), may hold values from -0.0625 to 0.0625
- live_token_count: int32 [8], P('dp'), may hold values from 128 to 384, as said below
- series_domain: int32 [8], replicated, may hold values from 0 to 3, as said below
Outputs:
- grad_input: bfloat16 [3072, 8192], P('dp', 'tensor')
- domain_down_gradient: float32 [4, 32, 8192], P(None, None, 'tensor')
- domain_up_gradient: float32 [4, 32, 8192], P(None, None, 'tensor')
- common_down_gradient: float32 [16, 8192], P(None, 'tensor')
- common_up_gradient: float32 [16, 8192], P(None, 'tensor')
Inputs may be any that keep to these rules, and one draw needn't show every extreme that they name: `live_token_count`: a multiple of 128; some series has exactly 384. `series_domain`: every domain is named by at least one series.
All inputs are finite; a program needn't handle non-finite values.
Results may differ from a plain program's by a relative error of at most 0.0035.
Values may be sent and summed in bfloat16 or wider, within the bound.
A program may use at most 128 MiB of HBM per device.

v0:
```python
import jax
import jax.numpy as jnp
from jax import lax
from jax.sharding import PartitionSpec as P

adapter_scale = 2.0
shared_scale = 2.0
contract_dims = (((1,), (1,)), ((), ()))
outer_dims = (((0,), (0,)), ((), ()))


def on_device(
    output_gradient,
    attention_output,
    frozen_projection,
    domain_down_map,
    domain_up_map,
    common_down_map,
    common_up_map,
    live_token_count,
    series_domain,
):
    rows_local = output_gradient.shape[0]
    tensor_index = lax.axis_index("tensor")
    rank_index = lax.axis_index("dp")
    domain_number = lax.dynamic_index_in_dim(series_domain, rank_index, 0, keepdims=False)
    local_down_map = lax.dynamic_index_in_dim(domain_down_map, domain_number, 0, keepdims=False)
    local_up_map = lax.dynamic_index_in_dim(domain_up_map, domain_number, 0, keepdims=False)
    positions = tensor_index * rows_local + lax.iota(jnp.int32, rows_local)
    live_rows = (positions < live_token_count[0])[:, None]
    masked = jnp.where(live_rows, output_gradient, jnp.zeros_like(output_gradient))
    down_part = lax.dot_general(
        attention_output, local_down_map, contract_dims, preferred_element_type=jnp.float32
    )
    shared_part = lax.dot_general(
        attention_output, common_down_map, contract_dims, preferred_element_type=jnp.float32
    )
    down_total, shared_total = lax.psum((down_part, shared_part), "tensor")
    reduced_activation = down_total.astype(jnp.bfloat16)
    low_shared = shared_total.astype(jnp.bfloat16)
    gathered = lax.all_gather(masked, "tensor", axis=0, tiled=True)
    column_width = local_up_map.shape[1]
    my_columns = lax.dynamic_slice_in_dim(gathered, tensor_index * column_width, column_width, 1)
    dom_partial = lax.dot_general(
        my_columns, local_up_map, contract_dims, preferred_element_type=jnp.float32
    )
    shared_partial = lax.dot_general(
        my_columns, common_up_map, contract_dims, preferred_element_type=jnp.float32
    )
    dom_total, shared_back_total = lax.psum((dom_partial, shared_partial), "tensor")
    domain_backward = dom_total.astype(jnp.bfloat16)
    back_shared = shared_back_total.astype(jnp.bfloat16)
    local_down_gradient = adapter_scale * lax.dot_general(
        domain_backward, attention_output, outer_dims, preferred_element_type=jnp.float32
    )
    local_up_gradient = adapter_scale * lax.dot_general(
        reduced_activation, my_columns, outer_dims, preferred_element_type=jnp.float32
    )
    grad_sdown = shared_scale * lax.dot_general(
        back_shared, attention_output, outer_dims, preferred_element_type=jnp.float32
    )
    grad_sup = shared_scale * lax.dot_general(
        low_shared, my_columns, outer_dims, preferred_element_type=jnp.float32
    )
    domain_picker = (lax.iota(jnp.int32, domain_down_map.shape[0]) == domain_number).astype(
        jnp.float32
    )[:, None, None]
    frozen_total = lax.dot_general(
        gathered,
        lax.all_gather(frozen_projection, "dp", axis=1, tiled=True),
        contract_dims,
        preferred_element_type=jnp.float32,
    )
    summed = lax.psum(
        (
            domain_picker * local_down_gradient[None],
            domain_picker * local_up_gradient[None],
            grad_sdown,
            grad_sup,
        ),
        "dp",
    )
    adapter_contribution = adapter_scale * jnp.dot(
        domain_backward, local_down_map, preferred_element_type=jnp.float32
    )
    adapter_contribution = adapter_contribution + shared_scale * jnp.dot(
        back_shared, common_down_map, preferred_element_type=jnp.float32
    )
    grad_input = (frozen_total + adapter_contribution).astype(jnp.bfloat16)
    return (grad_input, summed[0], summed[1], summed[2], summed[3])


def solution(mesh):
    placed = (
        P(("dp", "tensor"), None),
        P("dp", "tensor"),
        P("tensor", "dp"),
        P(None, None, "tensor"),
        P(None, None, "tensor"),
        P(None, "tensor"),
        P(None, "tensor"),
        P("dp"),
        P(),
    )
    return jax.shard_map(
        on_device,
        mesh=mesh,
        in_specs=placed,
        out_specs=(
            P("dp", "tensor"),
            P(None, None, "tensor"),
            P(None, None, "tensor"),
            P(None, "tensor"),
            P(None, "tensor"),
        ),
        check_vma=False,
    )
```

profile of v0, /device:TPU:0, one launch (start us, length us, event | category | flops | bytes accessed | tf_op | source)
XLA Modules:
  0.0 826.1 jit_solution(13282808707189045885)
XLA Ops:
  7.2 0.0 copy-start
  7.2 0.0 all-gather.3.cloned.1.call-start
  8.0 2.7 broadcast_select_fusion
  10.7 0.0 copy-start.6
  10.7 0.0 copy-start.1
  10.7 0.0 all-gather.3.cloned.1.call-update
  10.8 0.0 copy-start.4
  10.8 0.0 all-gather.5.cloned.1.call-start
  10.8 0.7 all-gather.5.cloned.1.call-update
  11.5 0.0 copy-start.5
  11.5 0.0 all-reduce.5.cloned.1.call-start
  11.6 0.0 copy-done.6
  11.6 0.6 dynamic_slice.15
  14.1 0.0 copy-done
  14.1 0.0 copy-done.1
  14.1 0.6 convolution_bitcast_fusion
  14.7 0.0 copy-done.4
  14.7 0.5 fusion.26
  15.3 0.7 compare_convert_fusion
  15.9 44.1 %all-gather.3.cloned.1.call-done = bf16[384,8192]{1,0:T(8,128)(2,1)} async-done(((bf16[96,8192]{1,0:T(8,128)(2,1)}), bf16[384,8192]{1,0:T(8,128)(2,1)}) %all-gather.3.cloned.1.call-update) | async-done | bytes 6291472 | tf_op jit(solution)/shard_map/all_gather | solution.py:41
  60.0 2.0 fusion.4
  62.0 0.0 copy-done.5
  62.0 1.9 fusion.2
  63.9 14.8 %all-reduce.6 = (bf16[384,32]{0,1:T(8,128)(2,1)S(1)}, bf16[384,16]{0,1:T(8,128)(2,1)S(1)}, bf16[384,32]{0,1:T(8,128)(2,1)S(1)}, bf16[384,16]{1,0:T(8,128)(2,1)S(1)}) all-reduce(f32[384,32]{0,1:T(8,128)S(1)} %fusion.4, f32[384,16]{0,1:T(8,128)S(1)} %fusion.2, ...), channel_id=1, replica_groups=mesh['dp'=8,'tensor'=4] {'tensor'}, use_global_device_ids=true, to_apply=%region_0.1 | all-reduce | flops 36864 | bytes 221184 | tf_op jit(solution)/shard_map/psum | solution.py:50
  78.7 2.4 convolution_multiply_fusion.2
  81.1 1.8 convolution_multiply_fusion
  82.9 1.0 convolution_multiply_fusion.3
  83.9 0.4 convolution_multiply_fusion.1
  84.3 2.3 fusion.7
  86.5 1.6 broadcast_multiply_fusion
  88.2 0.0 all-reduce.5.cloned.1.call-update
  88.2 611.1 %all-gather.5.cloned.1.call-done = bf16[2048,8192]{1,0:T(8,128)(2,1)} async-done(((bf16[2048,1024]{1,0:T(8,128)(2,1)}), bf16[2048,8192]{1,0:T(8,128)(2,1)}) %all-gather.5.cloned.1.call-update) | async-done | bytes 33554448 | tf_op jit(solution)/shard_map/all_gather | solution.py:70
  699.3 20.6 %fusion.25 = f32[384,2048]{1,0:T(8,128)} fusion(bf16[384,8192]{1,0:T(8,128)(2,1)} %all-gather.3.cloned.1.call-done, bf16[2048,8192]{1,0:T(8,128)(2,1)} %all-gather.5.cloned.1.call-done), kind=kOutput, calls=%fused_computation.36 | convolution fusion | flops 12884901888 | bytes 42991616 | tf_op jit(solution)/shard_map/dot_general | solution.py:68
  719.9 4.6 add_convert_fusion
  724.5 89.1 %all-reduce.5.cloned.1.call-done = (f32[4,32,2048]{2,1,0:T(8,128)}, f32[4,32,2048]{2,1,0:T(8,128)}, f32[16,2048]{1,0:T(8,128)}, f32[16,2048]{1,0:T(8,128)}) async-done(((f32[4,32,2048]{2,1,0:T(8,128)}, f32[4,32,2048]{2,1,0:T(8,128)}, f32[16,2048]{1,0:T(8,128)}, f32[16,2048]{1,0:T(8,128)}), (f32[4,32,2048]{2,1,0:T(8,128)}, f32[4,32,2048]{2,1,0:T(8,128)}, f32[16,2048]{1,0:T(8,128)}, ...) | async-done | bytes 2359312 | tf_op jit(solution)/shard_map/psum | solution.py:74
  813.6 0.0 copy-start.3
  813.6 0.0 copy-start.2
  813.6 2.3 copy.27
  815.9 2.3 copy.28
  818.2 0.0 copy-done.3
  818.2 0.7 copy.29
  818.9 0.0 copy-done.2
  818.9 0.7 copy.30
  (1 shorter events, 0.0 us)
Async XLA Ops:
  7.2 7.0 copy-start
  7.2 52.8 %all-gather.3.cloned.1.call-start = ((), (), s32[]{:S(2)}) async-start(), calls=%async_computation | async-start | bytes 7864320 | tf_op jit(solution)/shard_map/all_gather | solution.py:41
  10.7 0.9 copy-start.6
  10.7 3.4 copy-start.1
  10.8 4.0 copy-start.4
  10.8 688.5 %all-gather.5.cloned.1.call-start = ((), (), s32[]{:S(2)}) async-start(), calls=%async_computation.1 | async-start | bytes 37748736 | tf_op jit(solution)/shard_map/all_gather | solution.py:70
  11.5 50.5 %copy-start.5 = (bf16[16,2048]{1,0:T(8,128)(2,1)S(1)}, bf16[16,2048]{1,0:T(8,128)(2,1)}, u32[]{:S(2)}) copy-start(bf16[16,2048]{1,0:T(8,128)(2,1)} %param.15) | copy-start | bytes 196612
  11.5 802.0 %all-reduce.5.cloned.1.call-start = ((), (), s32[]{:S(2)}) async-start(), calls=%async_computation.2 | async-start | bytes 4718592 | tf_op jit(solution)/shard_map/psum | solution.py:74
  813.6 4.6 copy-start.3
  813.6 5.3 copy-start.2
Sparse Core Ops, SparseCore 0:
  10.9 49.0 all-gather.2
  61.5 637.7 all-gather.4
  703.7 109.8 all-reduce.4
where the time goes:
time: 826 us
  waiting for transfers between devices  745 us (90%)
  matrix products  38 us (5%)
  between operations  16.6 us (2%)
  blocking collectives  14.8 us (2%)
    all_gather x1, waiting for transfers between devices, on_device(): lax.all_gather(frozen_projection, 'dp', axis=1, tiled=True)  611 us
    psum x1, waiting for transfers between devices, on_device(): lax.psum((domain_picker * local_down_gradient[None], domain_picker * loca...  89.1 us
    all_gather x1, waiting for transfers between devices, on_device(): gathered = lax.all_gather(masked, 'tensor', axis=0, tiled=True)  44.1 us
    dot_general x1, matrix products, on_device(): lax.dot_general(gathered, lax.all_gather(frozen_projection, 'dp', axis=1,...  20.6 us
  transfers between devices with their start and end apart: 3, of which 3 were waited for; matrix products, arithmetic and copies ran while one was open for 5% of the time, Pallas kernels for 0%

commit v1 on v0

--- a/solution.py
+++ b/solution.py
@@ -1,6 +1,10 @@
+import functools
+
 import jax
 import jax.numpy as jnp
 from jax import lax
+from jax.experimental import pallas as pl
+from jax.experimental.pallas import tpu as pltpu
 from jax.sharding import PartitionSpec as P
 
 adapter_scale = 2.0
@@ -89,6 +93,445 @@
     grad_input = (frozen_total + adapter_contribution).astype(jnp.bfloat16)
     return (grad_input, summed[0], summed[1], summed[2], summed[3])
 
+MESH = pl.DeviceIdType.MESH
+CHUNK = 256
+
+
+def nt_dot(left, right):
+    return lax.dot_general(left, right, contract_dims, preferred_element_type=jnp.float32)
+
+
+def cube_kernel(
+    dims,
+    live_ref,
+    domain_ref,
+    grad_ref,
+    act_ref,
+    proj_ref,
+    dom_down_ref,
+    dom_up_ref,
+    com_down_ref,
+    com_up_ref,
+    out_ref,
+    down_grad_ref,
+    up_grad_ref,
+    sdown_ref,
+    sup_ref,
+    proj_other,
+    masked_blocks,
+    rows_all,
+    up_all,
+    down_map,
+    low_send,
+    low_recv,
+    back_all,
+    upg_send,
+    upg_recv,
+    sum_send,
+    sum_recv,
+    total_all,
+    zl_send,
+    zl_recv,
+    kept,
+    zh_send,
+    zh_recv,
+    proj_sems,
+    rowz_sems,
+    rowx_sems,
+    rowc_sems,
+    rowf_sems,
+    up_sems,
+    low_sems,
+    back_sems,
+    upg_sems,
+    sum_sems,
+    total_sems,
+    zl_sems,
+    zh_sems,
+):
+    n_dp, n_tensor, chunks = dims
+    dp = lax.axis_index("dp")
+    tensor = lax.axis_index("tensor")
+    y = lax.rem(dp, 2)
+    z = dp // 2
+    rows, block = masked_blocks.shape[1], masked_blocks.shape[2]
+    series_rows = rows * n_tensor
+    rank, srank = dom_down_ref.shape[1], com_down_ref.shape[0]
+    ranks = rank + srank
+    domains = dom_down_ref.shape[0]
+    width = act_ref.shape[1]
+    per_tensor = width // block
+    piece = width // n_dp
+
+    def flip(index, bit):
+        return index + bit - 2 * bit * lax.rem(index // bit, 2)
+
+    def flips(index, mask):
+        for bit in (1, 2, 4):
+            if mask & bit:
+                index = flip(index, bit)
+        return index
+
+    def copy(src, dst, sems, at, dp_to, tensor_to):
+        return pltpu.make_async_remote_copy(
+            src_ref=src,
+            dst_ref=dst,
+            send_sem=sems.at[0, at],
+            recv_sem=sems.at[1, at],
+            device_id=(dp_to, tensor_to),
+            device_id_type=MESH,
+        )
+
+    barrier = pltpu.get_barrier_semaphore()
+    for mask in range(1, n_dp):
+        pl.semaphore_signal(barrier, inc=1, device_id=(flips(dp, mask), tensor), device_id_type=MESH)
+    for mask in range(1, n_tensor):
+        pl.semaphore_signal(barrier, inc=1, device_id=(dp, flips(tensor, mask)), device_id_type=MESH)
+    pl.semaphore_wait(barrier, n_dp + n_tensor - 2)
+
+    def proj_copy(c):
+        at = pl.ds(pl.multiple_of(c * CHUNK, CHUNK), CHUNK)
+        return copy(proj_ref.at[at], proj_other.at[at], proj_sems, c, flip(dp, 1), tensor)
+
+    def row_z(m):
+        zt = flips(z, m)
+        return copy(
+            masked_blocks.at[pl.ds(zt * 2, 2)],
+            rows_all.at[m, tensor],
+            rowz_sems,
+            m - 1,
+            zt * 2 + y,
+            tensor,
+        )
+
+    def row_x(m):
+        here = rows_all.at[m, tensor]
+        return copy(here, here, rowx_sems, m, dp, flip(tensor, 2))
+
+    def row_core(m):
+        here = rows_all.at[m, tensor]
+        return copy(here, here, rowc_sems, m, dp, flip(tensor, 1))
+
+    def row_forward(m):
+        here = rows_all.at[m, flip(tensor, 2)]
+        return copy(here, here, rowf_sems, m, dp, flip(tensor, 1))
+
+    def up_copy(m):
+        here = up_all.at[tensor]
+        return copy(here, here, up_sems, m - 1, dp, flips(tensor, m))
+
+    def low_copy(m):
+        to = flips(tensor, m)
+        return copy(low_send.at[to], low_recv.at[m - 1], low_sems, m - 1, dp, to)
+
+    def back_copy(m):
+        here = back_all.at[tensor]
+        return copy(here, here, back_sems, m - 1, dp, flips(tensor, m))
+
+    def upg_copy(m):
+        to = flips(tensor, m)
+        return copy(upg_send.at[to], upg_recv.at[m - 1], upg_sems, m - 1, dp, to)
+
+    def sum_copy(m):
+        to = flips(dp, m)
+        return copy(sum_send.at[to], sum_recv.at[dp], sum_sems, m - 1, to, tensor)
+
+    def total_copy(held, bit):
+        here = total_all.at[flips(dp, held)]
+        return copy(here, here, total_sems, (held | bit) - 1, flip(dp, bit), tensor)
+
+    def zl_copy(c):
+        return copy(zl_send.at[c], zl_recv.at[c], zl_sems, c, flip(z, 1) * 2 + y, tensor)
+
+    def zh_copy(c):
+        return copy(zh_send.at[c], zh_recv.at[c], zh_sems, c, flip(z, 2) * 2 + y, tensor)
+
+    @pl.loop(0, chunks)
+    def _(c):
+        proj_copy(c).start()
+
+    live = live_ref[0]
+    alive = tensor * rows + lax.broadcasted_iota(jnp.int32, (rows, block), 0) < live
+    for j in range(masked_blocks.shape[0]):
+        part = grad_ref[:, j * block : (j + 1) * block]
+        masked_blocks[j] = jnp.where(alive, part, jnp.zeros_like(part))
+    for m in (3, 2, 1):
+        row_z(m).start()
+    for h in range(2):
+        rows_all[0, tensor, h] = masked_blocks[z * 2 + h]
+    row_x(0).start()
+    row_core(0).start()
+
+    domain = domain_ref[dp]
+    up_all[tensor, :rank] = dom_up_ref[domain]
+    up_all[tensor, rank:] = com_up_ref[...]
+    for m in range(1, n_tensor):
+        up_copy(m).start()
+    down_map[:rank] = dom_down_ref[domain]
+    down_map[rank:] = com_down_ref[...]
+    low_send[...] = jnp.zeros_like(low_send)
+    back_all[tensor] = jnp.zeros_like(back_all.at[0])
+    for j in range(n_tensor):
+        low_send[j, :, :ranks] = nt_dot(act_ref[j * rows : (j + 1) * rows, :], down_map[...])
+    for m in range(1, n_tensor):
+        low_copy(m).start()
+
+    for m in (1, 2, 3):
+        row_z(m).wait_recv()
+        row_x(m).start()
+        row_core(m).start()
+
+    for m in range(1, n_tensor):
+        up_copy(m).wait_recv()
+    back = jnp.zeros((rows, ranks), jnp.float32)
+    for j in range(masked_blocks.shape[0]):
+        at = (j % per_tensor) * block
+        back += nt_dot(masked_blocks[j], up_all[j // per_tensor, :, at : at + block])
+    back_all[tensor, :, :ranks] = back.astype(jnp.bfloat16)
+    for m in range(1, n_tensor):
+        back_copy(m).start()
+
+    low = low_send[tensor]
+    for m in range(1, n_tensor):
+        low_copy(m).wait_recv()
+        low += low_recv[m - 1]
+    low_flip = low.astype(jnp.bfloat16).astype(jnp.float32).T.astype(jnp.bfloat16)
+    for j in range(masked_blocks.shape[0]):
+        at = (j % per_tensor) * block
+        part = adapter_scale * jnp.dot(
+            low_flip, masked_blocks[j], preferred_element_type=jnp.float32
+        )
+        upg_send[j // per_tensor, :, at : at + block] = part[:ranks]
+    for m in range(1, n_tensor):
+        upg_copy(m).start()
+
+    for m in range(n_tensor):
+        row_x(m).wait_recv()
+        row_forward(m).start()
+
+    for m in range(1, n_tensor):
+        back_copy(m).wait_recv()
+    lanes = back_all.shape[2]
+    back_rows = back_all[...].reshape(series_rows, lanes)
+    back_flip = back_rows.astype(jnp.float32).T.astype(jnp.bfloat16)
+    for j in range(n_dp):
+        at = slice(j * piece, (j + 1) * piece)
+        part = adapter_scale * jnp.dot(
+            back_flip, act_ref[:, at], preferred_element_type=jnp.float32
+        )
+        sum_send[j, :ranks] = part[:ranks].astype(jnp.bfloat16)
+    for m in range(1, n_tensor):
+        upg_copy(m).wait_recv()
+    for j in range(n_dp):
+        at = slice(j * piece, (j + 1) * piece)
+        part = upg_send[tensor, :, at]
+        for m in range(1, n_tensor):
+            part += upg_recv[m - 1, :, at]
+        sum_send[j, ranks:] = part.astype(jnp.bfloat16)
+    for m in range(1, n_dp):
+        sum_copy(m).start()
+    sum_recv[dp] = sum_send[dp]
+
+    for m in range(n_tensor):
+        row_core(m).wait_recv()
+        row_forward(m).wait_recv()
+
+    def partial(m, c):
+        at = pl.ds(pl.multiple_of(c * CHUNK, CHUNK), CHUNK)
+        own = rows_all[m, :, y].reshape(series_rows, block)
+        other = rows_all[m, :, 1 - y].reshape(series_rows, block)
+        return nt_dot(own, proj_ref[at, :]) + nt_dot(other, proj_other[at, :])
+
+    def add_totals():
+        for m in range(1, n_dp):
+            sum_copy(m).wait_recv()
+        for kind in range(2):
+            base = kind * ranks
+            to = kind * (domains * rank + srank)
+            shared = jnp.zeros((srank, piece), jnp.float32)
+            for r in range(n_dp):
+                shared += sum_recv[r, base + rank : base + ranks].astype(jnp.float32)
+            for k in range(domains):
+                total = jnp.zeros((rank, piece), jnp.float32)
+                for r in range(n_dp):
+                    term = sum_recv[r, base : base + rank].astype(jnp.float32)
+                    total += jnp.where(domain_ref[r] == k, term, jnp.zeros_like(term))
+                total_all[dp, to + k * rank : to + (k + 1) * rank] = total.astype(jnp.bfloat16)
+            to += domains * rank
+            total_all[dp, to : to + srank] = shared.astype(jnp.bfloat16)
+
+    @pl.loop(0, chunks + 2)
+    def _(c):
+        @pl.when(c < chunks)
+        def _():
+            proj_copy(c).wait_recv()
+            zl_send[c, 0] = partial(1, c).astype(jnp.bfloat16)
+            zl_send[c, 1] = partial(3, c).astype(jnp.bfloat16)
+            zl_copy(c).start()
+            kept[c, 0] = partial(0, c)
+            kept[c, 1] = partial(2, c)
+
+        @pl.when(jnp.logical_and(c >= 1, c <= chunks))
+        def _():
+            b = c - 1
+            zl_copy(b).wait_recv()
+            zh_send[b] = (kept[b, 1] + zl_recv[b, 1].astype(jnp.float32)).astype(jnp.bfloat16)
+            zh_copy(b).start()
+
+        @pl.when(c >= 2)
+        def _():
+            a = c - 2
+            at = pl.ds(pl.multiple_of(a * CHUNK, CHUNK), CHUNK)
+            adapter = jnp.dot(
+                back_all[...].reshape(series_rows, lanes)[:, :ranks],
+                down_map[:, at],
+                preferred_element_type=jnp.float32,
+            )
+            whole = kept[a, 0] + zl_recv[a, 0].astype(jnp.float32) + adapter_scale * adapter
+            zh_copy(a).wait_recv()
+            out_ref[:, at] = (whole + zh_recv[a].astype(jnp.float32)).astype(jnp.bfloat16)
+
+        @pl.when(c == 1)
+        def _():
+            add_totals()
+            total_copy(0, 4).start()
+
+        @pl.when(c == 3)
+        def _():
+            total_copy(0, 4).wait_recv()
+            for held in (0, 4):
+                total_copy(held, 2).start()
+
+        @pl.when(c == 5)
+        def _():
+            for held in (0, 4):
+                total_copy(held, 2).wait_recv()
+            for held in (0, 2, 4, 6):
+                total_copy(held, 1).start()
+
+    for held in (0, 2, 4, 6):
+        total_copy(held, 1).wait_recv()
+    side = domains * rank + srank
+    for p in range(n_dp):
+        at = slice(p * piece, (p + 1) * piece)
+        for kind, dom_out, com_out in ((0, down_grad_ref, sdown_ref), (1, up_grad_ref, sup_ref)):
+            for k in range(domains):
+                first = kind * side + k * rank
+                dom_out[k, :, at] = total_all[p, first : first + rank].astype(jnp.float32)
+            first = kind * side + domains * rank
+            com_out[:, at] = total_all[p, first : first + srank].astype(jnp.float32)
+
+    @pl.loop(0, chunks)
+    def _(c):
+        proj_copy(c).wait_send()
+        zl_copy(c).wait_send()
+        zh_copy(c).wait_send()
+
+    for m in (1, 2, 3):
+        row_z(m).wait_send()
+    for m in range(n_tensor):
+        row_x(m).wait_send()
+        row_core(m).wait_send()
+        row_forward(m).wait_send()
+    for m in range(1, n_tensor):
+        up_copy(m).wait_send()
+        low_copy(m).wait_send()
+        back_copy(m).wait_send()
+        upg_copy(m).wait_send()
+    for m in range(1, n_dp):
+        sum_copy(m).wait_send()
+    for bit, helds in ((4, (0,)), (2, (0, 4)), (1, (0, 2, 4, 6))):
+        for held in helds:
+            total_copy(held, bit).wait_send()
+
+
+def on_cube(
+    n_dp,
+    n_tensor,
+    output_gradient,
+    attention_output,
+    frozen_projection,
+    domain_down_map,
+    domain_up_map,
+    common_down_map,
+    common_up_map,
+    live_token_count,
+    series_domain,
+):
+    rows, model = output_gradient.shape
+    series_rows, width = attention_output.shape
+    block = frozen_projection.shape[1]
+    domains, rank = domain_down_map.shape[:2]
+    srank = common_down_map.shape[0]
+    ranks, side = rank + srank, domains * rank + srank
+    chunks, piece, blocks = width // CHUNK, width // n_dp, model // block
+    lanes = 128
+    bf16, f32 = jnp.bfloat16, jnp.float32
+    vmem = pl.BlockSpec(memory_space=pltpu.VMEM)
+    smem = pl.BlockSpec(memory_space=pltpu.SMEM)
+
+    def sems(count):
+        return pltpu.SemaphoreType.DMA((2, count))
+
+    return pl.pallas_call(
+        functools.partial(cube_kernel, (n_dp, n_tensor, chunks)),
+        out_shape=(
+            jax.ShapeDtypeStruct((series_rows, width), bf16),
+            jax.ShapeDtypeStruct((domains, rank, width), f32),
+            jax.ShapeDtypeStruct((domains, rank, width), f32),
+            jax.ShapeDtypeStruct((srank, width), f32),
+            jax.ShapeDtypeStruct((srank, width), f32),
+        ),
+        in_specs=[smem] * 2 + [vmem] * 7,
+        out_specs=(vmem,) * 5,
+        scratch_shapes=[
+            pltpu.VMEM((width, block), bf16),
+            pltpu.VMEM((blocks, rows, block), bf16),
+            pltpu.VMEM((4, n_tensor, 2, rows, block), bf16),
+            pltpu.VMEM((n_tensor, ranks, width), bf16),
+            pltpu.VMEM((ranks, width), bf16),
+            pltpu.VMEM((n_tensor, rows, lanes), f32),
+            pltpu.VMEM((n_tensor - 1, rows, lanes), f32),
+            pltpu.VMEM((n_tensor, rows, lanes), bf16),
+            pltpu.VMEM((n_tensor, ranks, width), f32),
+            pltpu.VMEM((n_tensor - 1, ranks, width), f32),
+            pltpu.VMEM((n_dp, 2 * ranks, piece), bf16),
+            pltpu.VMEM((n_dp, 2 * ranks, piece), bf16),
+            pltpu.VMEM((n_dp, 2 * side, piece), bf16),
+            pltpu.VMEM((chunks, 2, series_rows, CHUNK), bf16),
+            pltpu.VMEM((chunks, 2, series_rows, CHUNK), bf16),
+            pltpu.VMEM((chunks, 2, series_rows, CHUNK), f32),
+            pltpu.VMEM((chunks, series_rows, CHUNK), bf16),
+            pltpu.VMEM((chunks, series_rows, CHUNK), bf16),
+            sems(chunks),
+            sems(3),
+            sems(n_tensor),
+            sems(n_tensor),
+            sems(n_tensor),
+            sems(n_tensor - 1),
+            sems(n_tensor - 1),
+            sems(n_tensor - 1),
+            sems(n_tensor - 1),
+            sems(n_dp - 1),
+            sems(n_dp - 1),
+            sems(chunks),
+            sems(chunks),
+        ],
+        compiler_params=pltpu.CompilerParams(
+            collective_id=0, has_side_effects=True, vmem_limit_bytes=60 * 1024 * 1024
+        ),
+    )(
+        live_token_count,
+        series_domain,
+        output_gradient,
+        attention_output,
+        frozen_projection,
+        domain_down_map,
+        domain_up_map,
+        common_down_map,
+        common_up_map,
+    )
+
 
 def solution(mesh):
     placed = (
@@ -102,8 +545,12 @@
         P("dp"),
         P(),
     )
+    n_dp, n_tensor = mesh.shape["dp"], mesh.shape["tensor"]
+    on_one = on_device
+    if n_dp == 2**3 and n_tensor == 2**2:
+        on_one = functools.partial(on_cube, n_dp, n_tensor)
     return jax.shard_map(
-        on_device,
+        on_one,
         mesh=mesh,
         in_specs=placed,
         out_specs=(

time: 826 us -> 215 us (0.26)
  waiting for transfers between devices: 745 us -> 0 us
  Pallas kernels: 0 us -> 207 us
  matrix products: 38 us -> 0 us
  between operations: 16.6 us -> 1.3 us
  blocking collectives: 14.8 us -> 0 us
    all_gather x2 -> x0, waiting for transfers between devices: 655 us -> none  [the longest x1 611 us: on_device(): lax.all_gather(frozen_projection, 'dp', axis=1, tiled=True)]
    pallas_call x0 -> x1, Pallas kernels: none -> 207 us  [on_cube(): pl.pallas_call(functools.partial(cube_kernel, (n_dp, n_tensor, chunks)),...]
    psum x1 -> x0, waiting for transfers between devices: 89.1 us -> none  [on_device(): lax.psum((domain_picker * local_down_gradient[None], domain_picker * loca...]
    dot_general x11 -> x0, matrix products: 38 us -> none  [the longest x1 20.6 us: on_device(): lax.dot_general(gathered, lax.all_gather(frozen_projection, 'dp', axis=1,...]
    psum x1 -> x0, blocking collectives: 14.8 us -> none  [on_device(): lax.psum((dom_partial, shared_partial), 'tensor')]
  transfers between devices with their start and end apart: 3 -> 0, of which waited for: 3 -> 0; matrix products, arithmetic and copies ran while one was open for 5% -> 0% of each run, Pallas kernels for 0% -> 0%
where the time goes in v1:
time: 215 us
  Pallas kernels  207 us (96%)
  local copies, waits for them, and re-layouts  6.71 us (3%)
    pallas_call x1, Pallas kernels, on_cube(): pl.pallas_call(functools.partial(cube_kernel, (n_dp, n_tensor, chunks)),...  207 us
    unnamed x13, local copies, waits for them, and re-layouts  6.71 us

profile of v1, /device:TPU:0, one launch (start us, length us, event | category | flops | bytes accessed | tf_op | source)
XLA Modules:
  0.0 215.2 jit_solution(4526612539623957991)
XLA Ops:
  1.3 207.2 %shard_map.128 = (bf16[384,2048]{1,0:T(8,128)(2,1)}, f32[4,32,2048]{2,1,0:T(8,128)}, f32[4,32,2048]{2,1,0:T(8,128)}, f32[16,2048]{1,0:T(8,128)}, f32[16,2048]{1,0:T(8,128)}) custom-call(s32[1]{0:T(128)S(6)} %copy.19.live_ref, s32[8]{0:T(128)} %domain_ref.1, bf16[96,8192]{1,0:T(8,128)(2,1)} %grad_ref.1, bf16[384,2048]{1,0:T(8,128)(2,1)} %act_ref.1, ...), custom_call_target="tpu_custom_call" | custom-call | tf_op jit(solution)/shard_map/pallas_call | solution.py:476
  208.5 0.0 copy-start.1
  208.5 2.8 %copy.20 = bf16[384,2048]{1,0:T(8,128)(2,1)} copy(bf16[384,2048]{1,0:T(8,128)(2,1)} %get-tuple-element.10) | data formatting | bytes 3145728
  211.4 0.0 copy-done.1
  211.4 0.0 copy-start
  211.4 0.0 copy-start.3
  211.4 1.0 copy.21
  212.3 0.6 copy-done
  213.0 0.0 copy-start.2
  213.0 1.0 copy.22
  213.9 0.0 copy-done.3
  213.9 0.7 copy.23
  214.6 0.0 copy-done.2
  214.6 0.7 copy.24
Async XLA Ops:
  208.5 2.8 %copy-start.1 = (f32[4,32,2048]{2,1,0:T(8,128)S(1)}, f32[4,32,2048]{2,1,0:T(8,128)}, u32[]{:S(2)}) copy-start(f32[4,32,2048]{2,1,0:T(8,128)} %get-tuple-element.11) | copy-start | bytes 3145732
  211.4 1.6 copy-start
  211.4 2.6 %copy-start.3 = (f32[16,2048]{1,0:T(8,128)S(1)}, f32[16,2048]{1,0:T(8,128)}, u32[]{:S(2)}) copy-start(f32[16,2048]{1,0:T(8,128)} %get-tuple-element.13) | copy-start | bytes 393220
  213.0 1.6 copy-start.2

commit v2 on v1

--- a/solution.py
+++ b/solution.py
@@ -95,6 +95,7 @@
 
 MESH = pl.DeviceIdType.MESH
 CHUNK = 256
+AHEAD = 2
 
 
 def nt_dot(left, right):
@@ -240,14 +241,38 @@
         here = total_all.at[flips(dp, held)]
         return copy(here, here, total_sems, (held | bit) - 1, flip(dp, bit), tensor)
 
-    def zl_copy(c):
-        return copy(zl_send.at[c], zl_recv.at[c], zl_sems, c, flip(z, 1) * 2 + y, tensor)
+    def zl_copy(k, c):
+        part_of = zl_send.at[c, k]
+        return copy(part_of, zl_recv.at[c, k], zl_sems, 2 * c + k, flip(z, 1) * 2 + y, tensor)
 
     def zh_copy(c):
         return copy(zh_send.at[c], zh_recv.at[c], zh_sems, c, flip(z, 2) * 2 + y, tensor)
 
-    @pl.loop(0, chunks)
-    def _(c):
+    def partial(m, c):
+        at = pl.ds(pl.multiple_of(c * CHUNK, CHUNK), CHUNK)
+        own = rows_all[m, :, y].reshape(series_rows, block)
+        other = rows_all[m, :, 1 - y].reshape(series_rows, block)
+        return nt_dot(own, proj_ref[at, :]) + nt_dot(other, proj_other[at, :])
+
+    def take_proj(c):
+        proj_copy(c).wait_recv()
+
+        @pl.when(c + AHEAD < chunks)
+        def _():
+            proj_copy(c).wait_send()
+            proj_copy(c + AHEAD).start()
+
+    def send_partial(k, c):
+        zl_send[c, k] = partial(2 * k + 1, c).astype(jnp.bfloat16)
+        zl_copy(k, c).start()
+
+    def finish_rows(m):
+        row_x(m).wait_recv()
+        row_forward(m).start()
+        row_core(m).wait_recv()
+        row_forward(m).wait_recv()
+
+    for c in range(AHEAD):
         proj_copy(c).start()
 
     live = live_ref[0]
@@ -255,8 +280,7 @@
     for j in range(masked_blocks.shape[0]):
         part = grad_ref[:, j * block : (j + 1) * block]
         masked_blocks[j] = jnp.where(alive, part, jnp.zeros_like(part))
-    for m in (3, 2, 1):
-        row_z(m).start()
+    row_z(1).start()
     for h in range(2):
         rows_all[0, tensor, h] = masked_blocks[z * 2 + h]
     row_x(0).start()
@@ -265,21 +289,35 @@
     domain = domain_ref[dp]
     up_all[tensor, :rank] = dom_up_ref[domain]
     up_all[tensor, rank:] = com_up_ref[...]
-    for m in range(1, n_tensor):
-        up_copy(m).start()
     down_map[:rank] = dom_down_ref[domain]
     down_map[rank:] = com_down_ref[...]
     low_send[...] = jnp.zeros_like(low_send)
     back_all[tensor] = jnp.zeros_like(back_all.at[0])
     for j in range(n_tensor):
         low_send[j, :, :ranks] = nt_dot(act_ref[j * rows : (j + 1) * rows, :], down_map[...])
+
+    row_z(1).wait_send()
+    row_z(3).start()
+    row_z(1).wait_recv()
+    row_x(1).start()
+    row_core(1).start()
     for m in range(1, n_tensor):
+        up_copy(m).start()
         low_copy(m).start()
-
-    for m in (1, 2, 3):
-        row_z(m).wait_recv()
-        row_x(m).start()
-        row_core(m).start()
+    row_x(0).wait_recv()
+    row_forward(0).start()
+    finish_rows(1)
+
+    take_proj(0)
+    send_partial(0, 0)
+    row_z(3).wait_send()
+    row_z(2).start()
+    take_proj(1)
+    send_partial(0, 1)
+
+    row_z(3).wait_recv()
+    row_x(3).start()
+    row_core(3).start()
 
     for m in range(1, n_tensor):
         up_copy(m).wait_recv()
@@ -302,45 +340,50 @@
             low_flip, masked_blocks[j], preferred_element_type=jnp.float32
         )
         upg_send[j // per_tensor, :, at : at + block] = part[:ranks]
+
+    finish_rows(3)
+    send_partial(1, 0)
+    send_partial(1, 1)
+    take_proj(2)
+    send_partial(0, 2)
+    send_partial(1, 2)
+    row_z(2).wait_recv()
+    row_x(2).start()
+    row_core(2).start()
     for m in range(1, n_tensor):
         upg_copy(m).start()
-
-    for m in range(n_tensor):
-        row_x(m).wait_recv()
-        row_forward(m).start()
-
-    for m in range(1, n_tensor):
-        back_copy(m).wait_recv()
+    take_proj(3)
+    send_partial(0, 3)
+    send_partial(1, 3)
+    finish_rows(2)
+    row_core(0).wait_recv()
+    row_forward(0).wait_recv()
+    early = 4
+
     lanes = back_all.shape[2]
-    back_rows = back_all[...].reshape(series_rows, lanes)
-    back_flip = back_rows.astype(jnp.float32).T.astype(jnp.bfloat16)
-    for j in range(n_dp):
-        at = slice(j * piece, (j + 1) * piece)
-        part = adapter_scale * jnp.dot(
-            back_flip, act_ref[:, at], preferred_element_type=jnp.float32
-        )
-        sum_send[j, :ranks] = part[:ranks].astype(jnp.bfloat16)
-    for m in range(1, n_tensor):
-        upg_copy(m).wait_recv()
-    for j in range(n_dp):
-        at = slice(j * piece, (j + 1) * piece)
-        part = upg_send[tensor, :, at]
+
+    def send_sums():
         for m in range(1, n_tensor):
-            part += upg_recv[m - 1, :, at]
-        sum_send[j, ranks:] = part.astype(jnp.bfloat16)
-    for m in range(1, n_dp):
-        sum_copy(m).start()
-    sum_recv[dp] = sum_send[dp]
-
-    for m in range(n_tensor):
-        row_core(m).wait_recv()
-        row_forward(m).wait_recv()
-
-    def partial(m, c):
-        at = pl.ds(pl.multiple_of(c * CHUNK, CHUNK), CHUNK)
-        own = rows_all[m, :, y].reshape(series_rows, block)
-        other = rows_all[m, :, 1 - y].reshape(series_rows, block)
-        return nt_dot(own, proj_ref[at, :]) + nt_dot(other, proj_other[at, :])
+            back_copy(m).wait_recv()
+        back_rows = back_all[...].reshape(series_rows, lanes)
+        back_flip = back_rows.astype(jnp.float32).T.astype(jnp.bfloat16)
+        for j in range(n_dp):
+            at = slice(j * piece, (j + 1) * piece)
+            part = adapter_scale * jnp.dot(
+                back_flip, act_ref[:, at], preferred_element_type=jnp.float32
+            )
+            sum_send[j, :ranks] = part[:ranks].astype(jnp.bfloat16)
+        for m in range(1, n_tensor):
+            upg_copy(m).wait_recv()
+        for j in range(n_dp):
+            at = slice(j * piece, (j + 1) * piece)
+            part = upg_send[tensor, :, at]
+            for m in range(1, n_tensor):
+                part += upg_recv[m - 1, :, at]
+            sum_send[j, ranks:] = part.astype(jnp.bfloat16)
+        for m in range(1, n_dp):
+            sum_copy(m).start()
+        sum_recv[dp] = sum_send[dp]
 
     def add_totals():
         for m in range(1, n_dp):
@@ -360,21 +403,34 @@
             to += domains * rank
             total_all[dp, to : to + srank] = shared.astype(jnp.bfloat16)
 
+    def write_totals():
+        side = domains * rank + srank
+        for p in range(n_dp):
+            at = slice(p * piece, (p + 1) * piece)
+            for kind, dom_out, com_out in ((0, down_grad_ref, sdown_ref), (1, up_grad_ref, sup_ref)):
+                for k in range(domains):
+                    first = kind * side + k * rank
+                    dom_out[k, :, at] = total_all[p, first : first + rank].astype(jnp.float32)
+                first = kind * side + domains * rank
+                com_out[:, at] = total_all[p, first : first + srank].astype(jnp.float32)
+
     @pl.loop(0, chunks + 2)
     def _(c):
+        @pl.when(jnp.logical_and(c >= early, c < chunks))
+        def _():
+            take_proj(c)
+            send_partial(0, c)
+            send_partial(1, c)
+
         @pl.when(c < chunks)
         def _():
-            proj_copy(c).wait_recv()
-            zl_send[c, 0] = partial(1, c).astype(jnp.bfloat16)
-            zl_send[c, 1] = partial(3, c).astype(jnp.bfloat16)
-            zl_copy(c).start()
+            kept[c, 1] = partial(2, c)
             kept[c, 0] = partial(0, c)
-            kept[c, 1] = partial(2, c)
 
         @pl.when(jnp.logical_and(c >= 1, c <= chunks))
         def _():
             b = c - 1
-            zl_copy(b).wait_recv()
+            zl_copy(1, b).wait_recv()
             zh_send[b] = (kept[b, 1] + zl_recv[b, 1].astype(jnp.float32)).astype(jnp.bfloat16)
             zh_copy(b).start()
 
@@ -387,48 +443,48 @@
                 down_map[:, at],
                 preferred_element_type=jnp.float32,
             )
+            zl_copy(0, a).wait_recv()
             whole = kept[a, 0] + zl_recv[a, 0].astype(jnp.float32) + adapter_scale * adapter
             zh_copy(a).wait_recv()
             out_ref[:, at] = (whole + zh_recv[a].astype(jnp.float32)).astype(jnp.bfloat16)
 
-        @pl.when(c == 1)
+        @pl.when(c == 0)
+        def _():
+            send_sums()
+
+        @pl.when(c == 2)
         def _():
             add_totals()
             total_copy(0, 4).start()
 
-        @pl.when(c == 3)
+        @pl.when(c == 4)
         def _():
             total_copy(0, 4).wait_recv()
             for held in (0, 4):
                 total_copy(held, 2).start()
 
-        @pl.when(c == 5)
+        @pl.when(c == 6)
         def _():
             for held in (0, 4):
                 total_copy(held, 2).wait_recv()
             for held in (0, 2, 4, 6):
                 total_copy(held, 1).start()
 
-    for held in (0, 2, 4, 6):
-        total_copy(held, 1).wait_recv()
-    side = domains * rank + srank
-    for p in range(n_dp):
-        at = slice(p * piece, (p + 1) * piece)
-        for kind, dom_out, com_out in ((0, down_grad_ref, sdown_ref), (1, up_grad_ref, sup_ref)):
-            for k in range(domains):
-                first = kind * side + k * rank
-                dom_out[k, :, at] = total_all[p, first : first + rank].astype(jnp.float32)
-            first = kind * side + domains * rank
-            com_out[:, at] = total_all[p, first : first + srank].astype(jnp.float32)
+        @pl.when(c == chunks)
+        def _():
+            for held in (0, 2, 4, 6):
+                total_copy(held, 1).wait_recv()
+            write_totals()
 
     @pl.loop(0, chunks)
     def _(c):
-        proj_copy(c).wait_send()
-        zl_copy(c).wait_send()
+        zl_copy(0, c).wait_send()
+        zl_copy(1, c).wait_send()
         zh_copy(c).wait_send()
 
-    for m in (1, 2, 3):
-        row_z(m).wait_send()
+    for c in range(AHEAD):
+        proj_copy(chunks - AHEAD + c).wait_send()
+    row_z(2).wait_send()
     for m in range(n_tensor):
         row_x(m).wait_send()
         row_core(m).wait_send()
@@ -514,7 +570,7 @@
             sems(n_tensor - 1),
             sems(n_dp - 1),
             sems(n_dp - 1),
-            sems(chunks),
+            sems(2 * chunks),
             sems(chunks),
         ],
         compiler_params=pltpu.CompilerParams(

time: 215 us -> 191 us (0.89); the launches traced: 215 us -> 188 us
  Pallas kernels: 207 us -> 180 us
    pallas_call x1, Pallas kernels: 207 us -> 180 us  [on_cube(): pl.pallas_call(functools.partial(cube_kernel, (n_dp, n_tensor, chunks)),...]
where the time goes in v2:
time: 191 us; the launch traced here: 188 us
  Pallas kernels  180 us (94%)
  local copies, waits for them, and re-layouts  6.71 us (4%)
    pallas_call x1, Pallas kernels, on_cube(): pl.pallas_call(functools.partial(cube_kernel, (n_dp, n_tensor, chunks)),...  180 us
    unnamed x13, local copies, waits for them, and re-layouts  6.71 us

profile of v2, /device:TPU:0, one launch (start us, length us, event | category | flops | bytes accessed | tf_op | source)
XLA Modules:
  0.0 187.5 jit_solution(12677586183338245418)
XLA Ops:
  1.3 179.5 %shard_map.128 = (bf16[384,2048]{1,0:T(8,128)(2,1)}, f32[4,32,2048]{2,1,0:T(8,128)}, f32[4,32,2048]{2,1,0:T(8,128)}, f32[16,2048]{1,0:T(8,128)}, f32[16,2048]{1,0:T(8,128)}) custom-call(s32[1]{0:T(128)S(6)} %copy.19.live_ref, s32[8]{0:T(128)} %domain_ref.1, bf16[96,8192]{1,0:T(8,128)(2,1)} %grad_ref.1, bf16[384,2048]{1,0:T(8,128)(2,1)} %act_ref.1, ...), custom_call_target="tpu_custom_call" | custom-call | tf_op jit(solution)/shard_map/pallas_call | solution.py:532
  180.8 0.0 copy-start.1
  180.8 2.8 %copy.20 = bf16[384,2048]{1,0:T(8,128)(2,1)} copy(bf16[384,2048]{1,0:T(8,128)(2,1)} %get-tuple-element.10) | data formatting | bytes 3145728
  183.6 0.0 copy-done.1
  183.6 0.0 copy-start
  183.6 0.0 copy-start.3
  183.7 1.0 copy.21
  184.6 0.6 copy-done
  185.3 0.0 copy-start.2
  185.3 1.0 copy.22
  186.2 0.0 copy-done.3
  186.2 0.7 copy.23
  186.9 0.0 copy-done.2
  186.9 0.7 copy.24
Async XLA Ops:
  180.8 2.8 %copy-start.1 = (f32[4,32,2048]{2,1,0:T(8,128)S(1)}, f32[4,32,2048]{2,1,0:T(8,128)}, u32[]{:S(2)}) copy-start(f32[4,32,2048]{2,1,0:T(8,128)} %get-tuple-element.11) | copy-start | bytes 3145732
  183.6 1.6 copy-start
  183.6 2.6 %copy-start.3 = (f32[16,2048]{1,0:T(8,128)S(1)}, f32[16,2048]{1,0:T(8,128)}, u32[]{:S(2)}) copy-start(f32[16,2048]{1,0:T(8,128)} %get-tuple-element.13) | copy-start | bytes 393220
  185.3 1.6 copy-start.2

commit v3 on v2

--- a/solution.py
+++ b/solution.py
@@ -95,7 +95,7 @@
 
 MESH = pl.DeviceIdType.MESH
 CHUNK = 256
-AHEAD = 2
+AHEAD = 3
 
 
 def nt_dot(left, right):
@@ -257,9 +257,10 @@
     def take_proj(c):
         proj_copy(c).wait_recv()
 
+        proj_copy(c).wait_send()
+
         @pl.when(c + AHEAD < chunks)
         def _():
-            proj_copy(c).wait_send()
             proj_copy(c + AHEAD).start()
 
     def send_partial(k, c):
@@ -272,7 +273,7 @@
         row_core(m).wait_recv()
         row_forward(m).wait_recv()
 
-    for c in range(AHEAD):
+    for c in range(AHEAD - 1):
         proj_copy(c).start()
 
     live = live_ref[0]
@@ -306,6 +307,7 @@
         low_copy(m).start()
     row_x(0).wait_recv()
     row_forward(0).start()
+    proj_copy(AHEAD - 1).start()
     finish_rows(1)
 
     take_proj(0)
@@ -350,12 +352,12 @@
     row_z(2).wait_recv()
     row_x(2).start()
     row_core(2).start()
-    for m in range(1, n_tensor):
-        upg_copy(m).start()
     take_proj(3)
     send_partial(0, 3)
     send_partial(1, 3)
     finish_rows(2)
+    for m in range(1, n_tensor):
+        upg_copy(m).start()
     row_core(0).wait_recv()
     row_forward(0).wait_recv()
     early = 4
@@ -416,11 +418,11 @@
 
     @pl.loop(0, chunks + 2)
     def _(c):
-        @pl.when(jnp.logical_and(c >= early, c < chunks))
-        def _():
-            take_proj(c)
-            send_partial(0, c)
-            send_partial(1, c)
+        @pl.when(c + early < chunks)
+        def _():
+            take_proj(c + early)
+            send_partial(0, c + early)
+            send_partial(1, c + early)
 
         @pl.when(c < chunks)
         def _():
@@ -448,11 +450,11 @@
             zh_copy(a).wait_recv()
             out_ref[:, at] = (whole + zh_recv[a].astype(jnp.float32)).astype(jnp.bfloat16)
 
-        @pl.when(c == 0)
+        @pl.when(c == 1)
         def _():
             send_sums()
 
-        @pl.when(c == 2)
+        @pl.when(c == 3)
         def _():
             add_totals()
             total_copy(0, 4).start()
@@ -463,7 +465,7 @@
             for held in (0, 4):
                 total_copy(held, 2).start()
 
-        @pl.when(c == 6)
+        @pl.when(c == 5)
         def _():
             for held in (0, 4):
                 total_copy(held, 2).wait_recv()
@@ -482,8 +484,6 @@
         zl_copy(1, c).wait_send()
         zh_copy(c).wait_send()
 
-    for c in range(AHEAD):
-        proj_copy(chunks - AHEAD + c).wait_send()
     row_z(2).wait_send()
     for m in range(n_tensor):
         row_x(m).wait_send()

time: 191 us -> 188 us (0.984)
  Pallas kernels: 180 us -> 177 us
    pallas_call x1, Pallas kernels: 180 us -> 177 us  [on_cube(): pl.pallas_call(functools.partial(cube_kernel, (n_dp, n_tensor, chunks)),...]
where the time goes in v3:
time: 188 us; the launch traced here: 185 us
  Pallas kernels  177 us (94%)
  local copies, waits for them, and re-layouts  6.71 us (4%)
    pallas_call x1, Pallas kernels, on_cube(): pl.pallas_call(functools.partial(cube_kernel, (n_dp, n_tensor, chunks)),...  177 us
    unnamed x13, local copies, waits for them, and re-layouts  6.71 us

profile of v3, /device:TPU:0, one launch (start us, length us, event | category | flops | bytes accessed | tf_op | source)
XLA Modules:
  0.0 184.8 jit_solution(14491736633362479357)
XLA Ops:
  1.3 176.8 %shard_map.128 = (bf16[384,2048]{1,0:T(8,128)(2,1)}, f32[4,32,2048]{2,1,0:T(8,128)}, f32[4,32,2048]{2,1,0:T(8,128)}, f32[16,2048]{1,0:T(8,128)}, f32[16,2048]{1,0:T(8,128)}) custom-call(s32[1]{0:T(128)S(6)} %copy.19.live_ref, s32[8]{0:T(128)} %domain_ref.1, bf16[96,8192]{1,0:T(8,128)(2,1)} %grad_ref.1, bf16[384,2048]{1,0:T(8,128)(2,1)} %act_ref.1, ...), custom_call_target="tpu_custom_call" | custom-call | tf_op jit(solution)/shard_map/pallas_call | solution.py:532
  178.0 0.0 copy-start.1
  178.1 2.8 %copy.20 = bf16[384,2048]{1,0:T(8,128)(2,1)} copy(bf16[384,2048]{1,0:T(8,128)(2,1)} %get-tuple-element.10) | data formatting | bytes 3145728
  180.9 0.0 copy-done.1
  180.9 0.0 copy-start
  180.9 0.0 copy-start.3
  180.9 1.0 copy.21
  181.8 0.6 copy-done
  182.5 0.0 copy-start.2
  182.5 1.0 copy.22
  183.4 0.0 copy-done.3
  183.4 0.7 copy.23
  184.1 0.0 copy-done.2
  184.1 0.7 copy.24
Async XLA Ops:
  178.0 2.8 %copy-start.1 = (f32[4,32,2048]{2,1,0:T(8,128)S(1)}, f32[4,32,2048]{2,1,0:T(8,128)}, u32[]{:S(2)}) copy-start(f32[4,32,2048]{2,1,0:T(8,128)} %get-tuple-element.11) | copy-start | bytes 3145732
  180.9 1.6 copy-start
  180.9 2.6 %copy-start.3 = (f32[16,2048]{1,0:T(8,128)S(1)}, f32[16,2048]{1,0:T(8,128)}, u32[]{:S(2)}) copy-start(f32[16,2048]{1,0:T(8,128)} %get-tuple-element.13) | copy-start | bytes 393220
  182.5 1.6 copy-start.2

commit v4 on v3

--- a/solution.py
+++ b/solution.py
@@ -114,10 +114,8 @@
     com_down_ref,
     com_up_ref,
     out_ref,
-    down_grad_ref,
-    up_grad_ref,
-    sdown_ref,
-    sup_ref,
+    adapters_ref,
+    proj_mine,
     proj_other,
     masked_blocks,
     rows_all,
@@ -133,9 +131,9 @@
     total_all,
     zl_send,
     zl_recv,
-    kept,
     zh_send,
     zh_recv,
+    mine_sem,
     proj_sems,
     rowz_sems,
     rowx_sems,
@@ -252,7 +250,7 @@
         at = pl.ds(pl.multiple_of(c * CHUNK, CHUNK), CHUNK)
         own = rows_all[m, :, y].reshape(series_rows, block)
         other = rows_all[m, :, 1 - y].reshape(series_rows, block)
-        return nt_dot(own, proj_ref[at, :]) + nt_dot(other, proj_other[at, :])
+        return nt_dot(own, proj_mine[at, :]) + nt_dot(other, proj_other[at, :])
 
     def take_proj(c):
         proj_copy(c).wait_recv()
@@ -275,6 +273,8 @@
 
     for c in range(AHEAD - 1):
         proj_copy(c).start()
+    mine = pltpu.make_async_copy(proj_ref, proj_mine, mine_sem)
+    mine.start()
 
     live = live_ref[0]
     alive = tensor * rows + lax.broadcasted_iota(jnp.int32, (rows, block), 0) < live
@@ -284,38 +284,38 @@
     row_z(1).start()
     for h in range(2):
         rows_all[0, tensor, h] = masked_blocks[z * 2 + h]
-    row_x(0).start()
-    row_core(0).start()
 
     domain = domain_ref[dp]
     up_all[tensor, :rank] = dom_up_ref[domain]
     up_all[tensor, rank:] = com_up_ref[...]
+    for m in range(1, n_tensor):
+        up_copy(m).start()
     down_map[:rank] = dom_down_ref[domain]
     down_map[rank:] = com_down_ref[...]
     low_send[...] = jnp.zeros_like(low_send)
     back_all[tensor] = jnp.zeros_like(back_all.at[0])
     for j in range(n_tensor):
         low_send[j, :, :ranks] = nt_dot(act_ref[j * rows : (j + 1) * rows, :], down_map[...])
+    for m in range(1, n_tensor):
+        low_copy(m).start()
 
     row_z(1).wait_send()
     row_z(3).start()
     row_z(1).wait_recv()
     row_x(1).start()
     row_core(1).start()
-    for m in range(1, n_tensor):
-        up_copy(m).start()
-        low_copy(m).start()
-    row_x(0).wait_recv()
-    row_forward(0).start()
     proj_copy(AHEAD - 1).start()
     finish_rows(1)
-
+    row_x(0).start()
+    row_core(0).start()
+
+    mine.wait()
     take_proj(0)
     send_partial(0, 0)
+    take_proj(1)
+    send_partial(0, 1)
     row_z(3).wait_send()
     row_z(2).start()
-    take_proj(1)
-    send_partial(0, 1)
 
     row_z(3).wait_recv()
     row_x(3).start()
@@ -341,8 +341,10 @@
         part = adapter_scale * jnp.dot(
             low_flip, masked_blocks[j], preferred_element_type=jnp.float32
         )
-        upg_send[j // per_tensor, :, at : at + block] = part[:ranks]
-
+        upg_send[j // per_tensor, :, at : at + block] = part[:ranks].astype(jnp.bfloat16)
+
+    for m in range(1, n_tensor):
+        upg_copy(m).start()
     finish_rows(3)
     send_partial(1, 0)
     send_partial(1, 1)
@@ -356,10 +358,7 @@
     send_partial(0, 3)
     send_partial(1, 3)
     finish_rows(2)
-    for m in range(1, n_tensor):
-        upg_copy(m).start()
-    row_core(0).wait_recv()
-    row_forward(0).wait_recv()
+    finish_rows(0)
     early = 4
 
     lanes = back_all.shape[2]
@@ -379,9 +378,9 @@
             upg_copy(m).wait_recv()
         for j in range(n_dp):
             at = slice(j * piece, (j + 1) * piece)
-            part = upg_send[tensor, :, at]
+            part = upg_send[tensor, :, at].astype(jnp.float32)
             for m in range(1, n_tensor):
-                part += upg_recv[m - 1, :, at]
+                part += upg_recv[m - 1, :, at].astype(jnp.float32)
             sum_send[j, ranks:] = part.astype(jnp.bfloat16)
         for m in range(1, n_dp):
             sum_copy(m).start()
@@ -406,35 +405,23 @@
             total_all[dp, to : to + srank] = shared.astype(jnp.bfloat16)
 
     def write_totals():
-        side = domains * rank + srank
         for p in range(n_dp):
-            at = slice(p * piece, (p + 1) * piece)
-            for kind, dom_out, com_out in ((0, down_grad_ref, sdown_ref), (1, up_grad_ref, sup_ref)):
-                for k in range(domains):
-                    first = kind * side + k * rank
-                    dom_out[k, :, at] = total_all[p, first : first + rank].astype(jnp.float32)
-                first = kind * side + domains * rank
-                com_out[:, at] = total_all[p, first : first + srank].astype(jnp.float32)
+            adapters_ref[:, p * piece : (p + 1) * piece] = total_all[p]
 
     @pl.loop(0, chunks + 2)
     def _(c):
+        @pl.when(c < chunks)
+        def _():
+            own = partial(2, c)
+            zl_copy(1, c).wait_recv()
+            zh_send[c] = (own + zl_recv[c, 1].astype(jnp.float32)).astype(jnp.bfloat16)
+            zh_copy(c).start()
+
         @pl.when(c + early < chunks)
         def _():
             take_proj(c + early)
             send_partial(0, c + early)
             send_partial(1, c + early)
-
-        @pl.when(c < chunks)
-        def _():
-            kept[c, 1] = partial(2, c)
-            kept[c, 0] = partial(0, c)
-
-        @pl.when(jnp.logical_and(c >= 1, c <= chunks))
-        def _():
-            b = c - 1
-            zl_copy(1, b).wait_recv()
-            zh_send[b] = (kept[b, 1] + zl_recv[b, 1].astype(jnp.float32)).astype(jnp.bfloat16)
-            zh_copy(b).start()
 
         @pl.when(c >= 2)
         def _():
@@ -445,9 +432,10 @@
                 down_map[:, at],
                 preferred_element_type=jnp.float32,
             )
+            whole = partial(0, a) + adapter_scale * adapter
             zl_copy(0, a).wait_recv()
-            whole = kept[a, 0] + zl_recv[a, 0].astype(jnp.float32) + adapter_scale * adapter
             zh_copy(a).wait_recv()
+            whole += zl_recv[a, 0].astype(jnp.float32)
             out_ref[:, at] = (whole + zh_recv[a].astype(jnp.float32)).astype(jnp.bfloat16)
 
         @pl.when(c == 1)
@@ -459,13 +447,13 @@
             add_totals()
             total_copy(0, 4).start()
 
-        @pl.when(c == 4)
+        @pl.when(c == 5)
         def _():
             total_copy(0, 4).wait_recv()
             for held in (0, 4):
                 total_copy(held, 2).start()
 
-        @pl.when(c == 5)
+        @pl.when(c == 6)
         def _():
             for held in (0, 4):
                 total_copy(held, 2).wait_recv()
@@ -529,18 +517,16 @@
     def sems(count):
         return pltpu.SemaphoreType.DMA((2, count))
 
-    return pl.pallas_call(
+    grad_input, adapters = pl.pallas_call(
         functools.partial(cube_kernel, (n_dp, n_tensor, chunks)),
         out_shape=(
             jax.ShapeDtypeStruct((series_rows, width), bf16),
-            jax.ShapeDtypeStruct((domains, rank, width), f32),
-            jax.ShapeDtypeStruct((domains, rank, width), f32),
-            jax.ShapeDtypeStruct((srank, width), f32),
-            jax.ShapeDtypeStruct((srank, width), f32),
+            jax.ShapeDtypeStruct((2 * side, width), bf16),
         ),
-        in_specs=[smem] * 2 + [vmem] * 7,
-        out_specs=(vmem,) * 5,
+        in_specs=[smem] * 2 + [vmem] * 2 + [pl.BlockSpec(memory_space=pl.ANY)] + [vmem] * 4,
+        out_specs=(vmem,) * 2,
         scratch_shapes=[
+            pltpu.VMEM((width, block), bf16),
             pltpu.VMEM((width, block), bf16),
             pltpu.VMEM((blocks, rows, block), bf16),
             pltpu.VMEM((4, n_tensor, 2, rows, block), bf16),
@@ -549,16 +535,16 @@
             pltpu.VMEM((n_tensor, rows, lanes), f32),
             pltpu.VMEM((n_tensor - 1, rows, lanes), f32),
             pltpu.VMEM((n_tensor, rows, lanes), bf16),
-            pltpu.VMEM((n_tensor, ranks, width), f32),
-            pltpu.VMEM((n_tensor - 1, ranks, width), f32),
+            pltpu.VMEM((n_tensor, ranks, width), bf16),
+            pltpu.VMEM((n_tensor - 1, ranks, width), bf16),
             pltpu.VMEM((n_dp, 2 * ranks, piece), bf16),
             pltpu.VMEM((n_dp, 2 * ranks, piece), bf16),
             pltpu.VMEM((n_dp, 2 * side, piece), bf16),
             pltpu.VMEM((chunks, 2, series_rows, CHUNK), bf16),
             pltpu.VMEM((chunks, 2, series_rows, CHUNK), bf16),
-            pltpu.VMEM((chunks, 2, series_rows, CHUNK), f32),
             pltpu.VMEM((chunks, series_rows, CHUNK), bf16),
             pltpu.VMEM((chunks, series_rows, CHUNK), bf16),
+            pltpu.SemaphoreType.DMA,
             sems(chunks),
             sems(3),
             sems(n_tensor),
@@ -587,6 +573,15 @@
         common_down_map,
         common_up_map,
     )
+    split = domains * rank
+    adapters = adapters.astype(f32)
+    return (
+        grad_input,
+        adapters[:split].reshape(domains, rank, width),
+        adapters[side : side + split].reshape(domains, rank, width),
+        adapters[split:side],
+        adapters[side + split :],
+    )
 
 
 def solution(mesh):

time: 188 us -> 180 us (0.957); the launches traced: 185 us -> 180 us
  Pallas kernels: 177 us -> 173 us
    unnamed x13 -> x3, local copies, waits for them, and re-layouts: 6.71 us -> 1.15 us
    slice x0 -> x2, local copies, waits for them, and re-layouts: none -> 4.47 us  [the longest x1 2.88 us: on_cube(): adapters[side:side + split].reshape(domains, rank, width)]
    pallas_call x1, Pallas kernels: 177 us -> 173 us  [on_cube(): pl.pallas_call(functools.partial(cube_kernel, (n_dp, n_tensor, chunks)),...]
where the time goes in v4:
time: 180 us
  Pallas kernels  173 us (96%)
  local copies, waits for them, and re-layouts  5.62 us (3%)
    pallas_call x1, Pallas kernels, on_cube(): pl.pallas_call(functools.partial(cube_kernel, (n_dp, n_tensor, chunks)),...  173 us

profile of v4, /device:TPU:0, one launch (start us, length us, event | category | flops | bytes accessed | tf_op | source)
XLA Modules:
  0.0 179.7 jit_solution(3078966032757348637)
XLA Ops:
  1.3 172.8 %shard_map.128 = (bf16[384,2048]{1,0:T(8,128)(2,1)}, bf16[288,2048]{1,0:T(8,128)(2,1)}) custom-call(s32[1]{0:T(128)S(6)} %copy.15.live_ref, s32[8]{0:T(128)} %domain_ref.1, bf16[96,8192]{1,0:T(8,128)(2,1)} %grad_ref.1, bf16[384,2048]{1,0:T(8,128)(2,1)} %act_ref.1, bf16[2048,1024]{1,0:T(8,128)(2,1)} %proj_ref.1, bf16[4,32,2048]{2,1,0:T(8,128)(2,1)} %dom_down_ref.1, ...), custom_call_target="tpu_custom_call" | custom-call | tf_op jit(solution)/shard_map/pallas_call | solution.py:520
  174.1 1.6 fusion
  175.7 0.0 copy-start
  175.7 2.9 %fusion.1 = (f32[128,2048]{1,0:T(8,128)}, f32[128,2048]{1,0:T(8,128)}) fusion(bf16[288,2048]{1,0:T(8,128)(2,1)} %get-tuple-element.8), kind=kLoop, calls=%fused_computation.1 | loop fusion | bytes 4194304 | tf_op jit(solution)/shard_map/slice | solution.py:581
  178.6 0.0 copy-done
  178.6 1.1 copy.16
Async XLA Ops:
  175.7 2.9 %copy-start = (bf16[384,2048]{1,0:T(8,128)(2,1)S(1)}, bf16[384,2048]{1,0:T(8,128)(2,1)}, u32[]{:S(2)}) copy-start(bf16[384,2048]{1,0:T(8,128)(2,1)} %get-tuple-element.18) | copy-start | bytes 4718596

commit v5 on v4

--- a/solution.py
+++ b/solution.py
@@ -192,28 +192,33 @@
         at = pl.ds(pl.multiple_of(c * CHUNK, CHUNK), CHUNK)
         return copy(proj_ref.at[at], proj_other.at[at], proj_sems, c, flip(dp, 1), tensor)
 
-    def row_z(m):
+    def row_z(m, h):
         zt = flips(z, m)
         return copy(
-            masked_blocks.at[pl.ds(zt * 2, 2)],
-            rows_all.at[m, tensor],
+            masked_blocks.at[zt * 2 + h],
+            rows_all.at[m, tensor, h],
             rowz_sems,
-            m - 1,
+            2 * (m - 1) + h,
             zt * 2 + y,
             tensor,
         )
 
-    def row_x(m):
-        here = rows_all.at[m, tensor]
-        return copy(here, here, rowx_sems, m, dp, flip(tensor, 2))
-
-    def row_core(m):
-        here = rows_all.at[m, tensor]
-        return copy(here, here, rowc_sems, m, dp, flip(tensor, 1))
-
-    def row_forward(m):
-        here = rows_all.at[m, flip(tensor, 2)]
-        return copy(here, here, rowf_sems, m, dp, flip(tensor, 1))
+    def row_x(m, h):
+        here = rows_all.at[m, tensor, h]
+        return copy(here, here, rowx_sems, 2 * m + h, dp, flip(tensor, 2))
+
+    def row_core(m, h):
+        here = rows_all.at[m, tensor, h]
+        return copy(here, here, rowc_sems, 2 * m + h, dp, flip(tensor, 1))
+
+    def row_forward(m, h):
+        here = rows_all.at[m, flip(tensor, 2), h]
+        return copy(here, here, rowf_sems, 2 * m + h, dp, flip(tensor, 1))
+
+    def share_rows(m):
+        for h in range(2):
+            row_x(m, h).start()
+            row_core(m, h).start()
 
     def up_copy(m):
         here = up_all.at[tensor]
@@ -266,13 +271,14 @@
         zl_copy(k, c).start()
 
     def finish_rows(m):
-        row_x(m).wait_recv()
-        row_forward(m).start()
-        row_core(m).wait_recv()
-        row_forward(m).wait_recv()
-
-    for c in range(AHEAD - 1):
-        proj_copy(c).start()
+        for h in range(2):
+            row_x(m, h).wait_recv()
+            row_forward(m, h).start()
+        for h in range(2):
+            row_core(m, h).wait_recv()
+            row_forward(m, h).wait_recv()
+
+    proj_copy(0).start()
     mine = pltpu.make_async_copy(proj_ref, proj_mine, mine_sem)
     mine.start()
 
@@ -281,7 +287,7 @@
     for j in range(masked_blocks.shape[0]):
         part = grad_ref[:, j * block : (j + 1) * block]
         masked_blocks[j] = jnp.where(alive, part, jnp.zeros_like(part))
-    row_z(1).start()
+    row_z(1, 0).start()
     for h in range(2):
         rows_all[0, tensor, h] = masked_blocks[z * 2 + h]
 
@@ -299,27 +305,36 @@
     for m in range(1, n_tensor):
         low_copy(m).start()
 
-    row_z(1).wait_send()
-    row_z(3).start()
-    row_z(1).wait_recv()
-    row_x(1).start()
-    row_core(1).start()
-    proj_copy(AHEAD - 1).start()
+    row_z(1, 0).wait_send()
+    row_z(1, 1).start()
+    row_z(1, 0).wait_recv()
+    row_x(1, 0).start()
+    row_core(1, 0).start()
+    row_z(1, 1).wait_send()
+    for h in range(2):
+        row_z(3, h).start()
+    row_z(1, 1).wait_recv()
+    row_x(1, 1).start()
+    row_core(1, 1).start()
+    proj_copy(1).start()
     finish_rows(1)
-    row_x(0).start()
-    row_core(0).start()
+    share_rows(0)
+    for c in range(2, AHEAD):
+        proj_copy(c).start()
 
     mine.wait()
     take_proj(0)
     send_partial(0, 0)
     take_proj(1)
     send_partial(0, 1)
-    row_z(3).wait_send()
-    row_z(2).start()
-
-    row_z(3).wait_recv()
-    row_x(3).start()
-    row_core(3).start()
+    for h in range(2):
+        row_z(3, h).wait_send()
+    for h in range(2):
+        row_z(2, h).start()
+
+    for h in range(2):
+        row_z(3, h).wait_recv()
+    share_rows(3)
 
     for m in range(1, n_tensor):
         up_copy(m).wait_recv()
@@ -351,9 +366,9 @@
     take_proj(2)
     send_partial(0, 2)
     send_partial(1, 2)
-    row_z(2).wait_recv()
-    row_x(2).start()
-    row_core(2).start()
+    for h in range(2):
+        row_z(2, h).wait_recv()
+    share_rows(2)
     take_proj(3)
     send_partial(0, 3)
     send_partial(1, 3)
@@ -472,11 +487,12 @@
         zl_copy(1, c).wait_send()
         zh_copy(c).wait_send()
 
-    row_z(2).wait_send()
-    for m in range(n_tensor):
-        row_x(m).wait_send()
-        row_core(m).wait_send()
-        row_forward(m).wait_send()
+    for h in range(2):
+        row_z(2, h).wait_send()
+        for m in range(n_tensor):
+            row_x(m, h).wait_send()
+            row_core(m, h).wait_send()
+            row_forward(m, h).wait_send()
     for m in range(1, n_tensor):
         up_copy(m).wait_send()
         low_copy(m).wait_send()
@@ -487,6 +503,18 @@
     for bit, helds in ((4, (0,)), (2, (0, 4)), (1, (0, 2, 4, 6))):
         for held in helds:
             total_copy(held, bit).wait_send()
+
+
+def widen_kernel(grad_ref, sums_ref, grad_out, down_out, up_out, sdown_out, sup_out):
+    grad_out[...] = grad_ref[...]
+    domains, rank = down_out.shape[:2]
+    first = 0
+    for dom_out, com_out in ((down_out, sdown_out), (up_out, sup_out)):
+        for k in range(domains):
+            dom_out[k] = sums_ref[first : first + rank].astype(jnp.float32)
+            first += rank
+        com_out[...] = sums_ref[first : first + com_out.shape[0]].astype(jnp.float32)
+        first += com_out.shape[0]
 
 
 def on_cube(
@@ -546,10 +574,10 @@
             pltpu.VMEM((chunks, series_rows, CHUNK), bf16),
             pltpu.SemaphoreType.DMA,
             sems(chunks),
-            sems(3),
-            sems(n_tensor),
-            sems(n_tensor),
-            sems(n_tensor),
+            sems(2 * 3),
+            sems(2 * n_tensor),
+            sems(2 * n_tensor),
+            sems(2 * n_tensor),
             sems(n_tensor - 1),
             sems(n_tensor - 1),
             sems(n_tensor - 1),
@@ -573,15 +601,32 @@
         common_down_map,
         common_up_map,
     )
-    split = domains * rank
-    adapters = adapters.astype(f32)
-    return (
-        grad_input,
-        adapters[:split].reshape(domains, rank, width),
-        adapters[side : side + split].reshape(domains, rank, width),
-        adapters[split:side],
-        adapters[side + split :],
-    )
+    strip = width // 4
+
+    def strips(*lead):
+        shape = (*lead, strip)
+        return pl.BlockSpec(shape, lambda i: (0,) * len(lead) + (i,))
+
+    return pl.pallas_call(
+        widen_kernel,
+        grid=(width // strip,),
+        out_shape=(
+            jax.ShapeDtypeStruct((series_rows, width), bf16),
+            jax.ShapeDtypeStruct((domains, rank, width), f32),
+            jax.ShapeDtypeStruct((domains, rank, width), f32),
+            jax.ShapeDtypeStruct((srank, width), f32),
+            jax.ShapeDtypeStruct((srank, width), f32),
+        ),
+        in_specs=[strips(series_rows), strips(2 * side)],
+        out_specs=(
+            strips(series_rows),
+            strips(domains, rank),
+            strips(domains, rank),
+            strips(srank),
+            strips(srank),
+        ),
+        compiler_params=pltpu.CompilerParams(vmem_limit_bytes=32 * 1024 * 1024),
+    )(grad_input, adapters)
 
 
 def solution(mesh):

time: 180 us -> 179 us (level)
  local copies, waits for them, and re-layouts: 5.62 us -> 2.67 us
  Pallas kernels: 173 us -> 175 us
    slice x2 -> x0, local copies, waits for them, and re-layouts: 4.47 us -> none  [the longest x1 2.88 us: on_cube(): adapters[side:side + split].reshape(domains, rank, width)]
    pallas_call x0 -> x1, Pallas kernels: none -> 2.48 us  [on_cube(): pl.pallas_call(widen_kernel, grid=(width // strip,), out_shape=(jax.Shape...]
where the time goes in v5:
time: 179 us
  Pallas kernels  175 us (98%)
  local copies, waits for them, and re-layouts  2.67 us (1%)
    pallas_call x1, Pallas kernels, on_cube(): pl.pallas_call(functools.partial(cube_kernel, (n_dp, n_tensor, chunks)),...  173 us

profile of v5, /device:TPU:0, one launch (start us, length us, event | category | flops | bytes accessed | tf_op | source)
XLA Modules:
  0.0 179.1 jit_solution(17767518136061797513)
XLA Ops:
  1.3 172.6 %shard_map.128 = (bf16[384,2048]{1,0:T(8,128)(2,1)}, bf16[288,2048]{1,0:T(8,128)(2,1)}) custom-call(s32[1]{0:T(128)S(6)} %copy.14.live_ref, s32[8]{0:T(128)} %domain_ref.1, bf16[96,8192]{1,0:T(8,128)(2,1)} %grad_ref.1, bf16[384,2048]{1,0:T(8,128)(2,1)} %act_ref.1, bf16[2048,1024]{1,0:T(8,128)(2,1)} %proj_ref.1, bf16[4,32,2048]{2,1,0:T(8,128)(2,1)} %dom_down_ref.1, ...), custom_call_target="tpu_custom_call" | custom-call | tf_op jit(solution)/shard_map/pallas_call | solution.py:548
  173.9 0.0 copy-start
  173.9 1.4 copy-done
  175.3 0.0 copy-start.1
  175.3 1.3 copy-done.1
  176.6 2.5 %shard_map.129 = (bf16[384,2048]{1,0:T(8,128)(2,1)}, f32[4,32,2048]{2,1,0:T(8,128)}, f32[4,32,2048]{2,1,0:T(8,128)}, f32[16,2048]{1,0:T(8,128)}, f32[16,2048]{1,0:T(8,128)}) custom-call(bf16[384,2048]{1,0:T(8,128)(2,1)S(1)} %copy-done, bf16[288,2048]{1,0:T(8,128)(2,1)S(1)} %copy-done.1), custom_call_target="tpu_custom_call" | custom-call | tf_op jit(solution)/shard_map/pallas_call | solution.py:610
Async XLA Ops:
  173.9 1.4 copy-start
  175.3 1.3 copy-start.1

commit v6 on v5

--- a/solution.py
+++ b/solution.py
@@ -96,6 +96,7 @@
 MESH = pl.DeviceIdType.MESH
 CHUNK = 256
 AHEAD = 3
+LATER = 2
 
 
 def nt_dot(left, right):
@@ -435,8 +436,11 @@
         @pl.when(c + early < chunks)
         def _():
             take_proj(c + early)
-            send_partial(0, c + early)
             send_partial(1, c + early)
+
+        @pl.when(jnp.logical_and(c + LATER >= early, c + LATER < chunks))
+        def _():
+            send_partial(0, c + LATER)
 
         @pl.when(c >= 2)
         def _():
@@ -453,29 +457,29 @@
             whole += zl_recv[a, 0].astype(jnp.float32)
             out_ref[:, at] = (whole + zh_recv[a].astype(jnp.float32)).astype(jnp.bfloat16)
 
-        @pl.when(c == 1)
+        @pl.when(c == 0)
         def _():
             send_sums()
 
-        @pl.when(c == 3)
+        @pl.when(c == 4)
         def _():
             add_totals()
             total_copy(0, 4).start()
 
-        @pl.when(c == 5)
+        @pl.when(c == 6)
         def _():
             total_copy(0, 4).wait_recv()
             for held in (0, 4):
                 total_copy(held, 2).start()
 
-        @pl.when(c == 6)
+        @pl.when(c == 7)
         def _():
             for held in (0, 4):
                 total_copy(held, 2).wait_recv()
             for held in (0, 2, 4, 6):
                 total_copy(held, 1).start()
 
-        @pl.when(c == chunks)
+        @pl.when(c == chunks + 1)
         def _():
             for held in (0, 2, 4, 6):
                 total_copy(held, 1).wait_recv()
@@ -625,7 +629,7 @@
             strips(srank),
             strips(srank),
         ),
-        compiler_params=pltpu.CompilerParams(vmem_limit_bytes=32 * 1024 * 1024),
+        compiler_params=pltpu.CompilerParams(vmem_limit_bytes=60 * 1024 * 1024),
     )(grad_input, adapters)
 
 

time: 179 us -> 182 us (1.017)
  Pallas kernels: 175 us -> 180 us
  local copies, waits for them, and re-layouts: 2.67 us -> 0 us
    pallas_call x1, Pallas kernels: 173 us -> 176 us  [on_cube(): pl.pallas_call(functools.partial(cube_kernel, (n_dp, n_tensor, chunks)),...]
    unnamed x4 -> x0, local copies, waits for them, and re-layouts: 2.67 us -> none
where the time goes in v6:
time: 182 us
  Pallas kernels  180 us (99%)
    pallas_call x1, Pallas kernels, on_cube(): pl.pallas_call(functools.partial(cube_kernel, (n_dp, n_tensor, chunks)),...  176 us
    pallas_call x1, Pallas kernels, on_cube(): pl.pallas_call(widen_kernel, grid=(width // strip,), out_shape=(jax.Shape...  4.21 us

profile of v6, /device:TPU:0, one launch (start us, length us, event | category | flops | bytes accessed | tf_op | source)
XLA Modules:
  0.0 181.6 jit_solution(1804204353041953421)
XLA Ops:
  1.3 176.1 %shard_map.128 = (bf16[384,2048]{1,0:T(8,128)(2,1)}, bf16[288,2048]{1,0:T(8,128)(2,1)}) custom-call(s32[1]{0:T(128)S(6)} %copy.14.live_ref, s32[8]{0:T(128)} %domain_ref.1, bf16[96,8192]{1,0:T(8,128)(2,1)} %grad_ref.1, bf16[384,2048]{1,0:T(8,128)(2,1)} %act_ref.1, bf16[2048,1024]{1,0:T(8,128)(2,1)} %proj_ref.1, bf16[4,32,2048]{2,1,0:T(8,128)(2,1)} %dom_down_ref.1, ...), custom_call_target="tpu_custom_call" | custom-call | tf_op jit(solution)/shard_map/pallas_call | solution.py:552
  177.4 4.2 %shard_map.129 = (bf16[384,2048]{1,0:T(8,128)(2,1)}, f32[4,32,2048]{2,1,0:T(8,128)}, f32[4,32,2048]{2,1,0:T(8,128)}, f32[16,2048]{1,0:T(8,128)}, f32[16,2048]{1,0:T(8,128)}) custom-call(bf16[384,2048]{1,0:T(8,128)(2,1)} %get-tuple-element.7.grad_ref, bf16[288,2048]{1,0:T(8,128)(2,1)} %get-tuple-element.8.sums_ref), custom_call_target="tpu_custom_call" | custom-call | tf_op jit(solution)/shard_map/pallas_call | solution.py:614

commit v7 on v5

--- a/solution.py
+++ b/solution.py
@@ -215,10 +215,9 @@
         here = rows_all.at[m, flip(tensor, 2), h]
         return copy(here, here, rowf_sems, 2 * m + h, dp, flip(tensor, 1))
 
-    def share_rows(m):
-        for h in range(2):
-            row_x(m, h).start()
-            row_core(m, h).start()
+    def share_half(m, h):
+        row_x(m, h).start()
+        row_core(m, h).start()
 
     def up_copy(m):
         here = up_all.at[tensor]
@@ -288,6 +287,8 @@
         part = grad_ref[:, j * block : (j + 1) * block]
         masked_blocks[j] = jnp.where(alive, part, jnp.zeros_like(part))
     row_z(1, 0).start()
+    for h in range(2):
+        row_z(3, h).start()
     for h in range(2):
         rows_all[0, tensor, h] = masked_blocks[z * 2 + h]
 
@@ -311,30 +312,27 @@
     row_x(1, 0).start()
     row_core(1, 0).start()
     row_z(1, 1).wait_send()
-    for h in range(2):
-        row_z(3, h).start()
     row_z(1, 1).wait_recv()
     row_x(1, 1).start()
     row_core(1, 1).start()
     proj_copy(1).start()
     finish_rows(1)
-    share_rows(0)
     for c in range(2, AHEAD):
         proj_copy(c).start()
 
+    for h in range(2):
+        row_z(3, h).wait_send()
+    for h in range(2):
+        row_z(2, h).start()
     mine.wait()
     take_proj(0)
     send_partial(0, 0)
     take_proj(1)
     send_partial(0, 1)
-    for h in range(2):
-        row_z(3, h).wait_send()
-    for h in range(2):
-        row_z(2, h).start()
 
     for h in range(2):
         row_z(3, h).wait_recv()
-    share_rows(3)
+        share_half(3, h)
 
     for m in range(1, n_tensor):
         up_copy(m).wait_recv()
@@ -368,12 +366,13 @@
     send_partial(1, 2)
     for h in range(2):
         row_z(2, h).wait_recv()
-    share_rows(2)
+        share_half(2, h)
     take_proj(3)
     send_partial(0, 3)
     send_partial(1, 3)
     finish_rows(2)
-    finish_rows(0)
+    for h in range(2):
+        share_half(0, h)
     early = 4
 
     lanes = back_all.shape[2]
@@ -455,6 +454,7 @@
 
         @pl.when(c == 1)
         def _():
+            finish_rows(0)
             send_sums()
 
         @pl.when(c == 3)
@@ -625,7 +625,7 @@
             strips(srank),
             strips(srank),
         ),
-        compiler_params=pltpu.CompilerParams(vmem_limit_bytes=32 * 1024 * 1024),
+        compiler_params=pltpu.CompilerParams(vmem_limit_bytes=60 * 1024 * 1024),
     )(grad_input, adapters)
 
 

time: 179 us -> 185 us (1.034)
  Pallas kernels: 175 us -> 184 us
  local copies, waits for them, and re-layouts: 2.67 us -> 0 us
    pallas_call x1, Pallas kernels: 173 us -> 180 us  [on_cube(): pl.pallas_call(functools.partial(cube_kernel, (n_dp, n_tensor, chunks)),...]
    unnamed x4 -> x0, local copies, waits for them, and re-layouts: 2.67 us -> none
where the time goes in v7:
time: 185 us
  Pallas kernels  184 us (99%)
    pallas_call x1, Pallas kernels, on_cube(): pl.pallas_call(functools.partial(cube_kernel, (n_dp, n_tensor, chunks)),...  180 us
    pallas_call x1, Pallas kernels, on_cube(): pl.pallas_call(widen_kernel, grid=(width // strip,), out_shape=(jax.Shape...  4.21 us

profile of v7, /device:TPU:0, one launch (start us, length us, event | category | flops | bytes accessed | tf_op | source)
XLA Modules:
  0.0 185.2 jit_solution(9782302382836117233)
XLA Ops:
  1.3 179.7 %shard_map.128 = (bf16[384,2048]{1,0:T(8,128)(2,1)}, bf16[288,2048]{1,0:T(8,128)(2,1)}) custom-call(s32[1]{0:T(128)S(6)} %copy.14.live_ref, s32[8]{0:T(128)} %domain_ref.1, bf16[96,8192]{1,0:T(8,128)(2,1)} %grad_ref.1, bf16[384,2048]{1,0:T(8,128)(2,1)} %act_ref.1, bf16[2048,1024]{1,0:T(8,128)(2,1)} %proj_ref.1, bf16[4,32,2048]{2,1,0:T(8,128)(2,1)} %dom_down_ref.1, ...), custom_call_target="tpu_custom_call" | custom-call | tf_op jit(solution)/shard_map/pallas_call | solution.py:548
  181.0 4.2 %shard_map.129 = (bf16[384,2048]{1,0:T(8,128)(2,1)}, f32[4,32,2048]{2,1,0:T(8,128)}, f32[4,32,2048]{2,1,0:T(8,128)}, f32[16,2048]{1,0:T(8,128)}, f32[16,2048]{1,0:T(8,128)}) custom-call(bf16[384,2048]{1,0:T(8,128)(2,1)} %get-tuple-element.7.grad_ref, bf16[288,2048]{1,0:T(8,128)(2,1)} %get-tuple-element.8.sums_ref), custom_call_target="tpu_custom_call" | custom-call | tf_op jit(solution)/shard_map/pallas_call | solution.py:610
